TPU v7x, 512 devices: a whole 4x4x16 slice. The times are simulated.
512 devices in a mesh: tile: 8 (over y, core), depth: 64 (over x, z).
Axes of the slice: x: 4, y: 4, z: 16, core: 2. Of those that a mesh axis runs over, the one named last changes fastest.
Arguments:
- density: float32 [128, 2048, 2048], P('tile', 'depth'), may hold values from 0.2 to 3
- slab_start: int32 [16, 64, 16], P('tile', 'depth'), may hold values from 0 to 31, as said below
- slab_count: int32 [16, 64, 16], P('tile', 'depth'), may hold values from 1 to 32
- emission: float32 [3], replicated, may hold values from 0.5 to 2
- extinction: float32 [1], replicated, may hold values from 1 to 4
- edge_gain: float32 [1], replicated, may hold values from 0.25 to 1
Outputs:
- image: float32 [4, 128, 2048], P(None, 'tile')
Inputs may be any that keep to these rules, and one draw needn't show every extreme that they name: `slab_start`: start + count of each brick is at most 32.
All inputs are finite; a program needn't handle non-finite values.
Results may differ from a plain program's by a relative error of at most 0.0003.
Values sent between devices are 32-bit elements; how exact they have to be, the bound alone decides.
A program may use at most 128 MiB of HBM per device.

v0:
```python
import jax
import jax.numpy as jnp
from jax import lax
from jax.sharding import PartitionSpec as P


def padded_2(shard, sides, width):
    for axis, dim in sides:
        size, length = (lax.axis_size(axis), shard.shape[dim])
        up = [(i, (i + 1) % size) for i in range(size - 1)]
        down = [(j, i) for i, j in up]
        last = lax.slice_in_dim(shard, length - width, length, axis=dim)
        leading = lax.slice_in_dim(shard, 0, width, axis=dim)
        before = lax.ppermute(last, axis, up)
        after = lax.ppermute(leading, axis, down)
        shard = jnp.concatenate([before, shard, after], axis=dim)
    return shard


def from_partner(value, axis, stride):
    mask = 2**stride
    pairs = [(source, source ^ mask) for source in range(lax.axis_size(axis))]
    return lax.ppermute(value, axis, pairs)


def expand_local(table, rows, width):
    row_bricks = table.shape[0]
    col_bricks = table.shape[2]
    flat = table[:, 0, :]
    spread = jnp.broadcast_to(
        flat[:, None, :, None], (row_bricks, rows // row_bricks, col_bricks, width // col_bricks)
    )
    return spread.reshape(rows, width)


def composite(front, back):
    return jnp.concatenate([front[:3] + front[3:4] * back[:3], front[3:4] * back[3:4]], axis=0)


def shards(density, slab_start, slab_count, emission, extinction, edge_gain):
    rows, slices, width = density.shape
    depth_count = lax.axis_size("depth")
    depth_total = slices * depth_count
    low = expand_local(slab_start, rows, width)
    high = expand_local(slab_start + slab_count, rows, width)
    padded = padded_2(density, (("tile", 0),), 1)

    def march(k, carry):
        color, trans = carry
        live = ((low <= k) & (k < high)).astype(jnp.float32)
        column = lax.dynamic_index_in_dim(padded, k, 1, keepdims=False)
        dens = column[1:-1]
        grad_y = (column[2:] - column[:-2]) * 0.5
        side = jnp.pad(dens, ((0, 0), (1, 1)))
        grad_x = (side[:, 2:] - side[:, :-2]) * 0.5
        source = dens + edge_gain[0] * (grad_y * grad_y + grad_x * grad_x)
        tau = extinction[0] * dens * live / depth_total
        keep = jnp.exp(-tau)
        weight = trans * (1.0 - keep) * source
        color = color + weight[None] * emission[:, None, None]
        return (color, trans * keep)

    init = (jnp.zeros((3, rows, width), jnp.float32), jnp.ones((rows, width), jnp.float32))
    color, trans = lax.fori_loop(0, slices, march, init)
    pixels = rows * width
    state = jnp.concatenate([color.reshape(3, pixels), trans.reshape(1, pixels)], axis=0)
    levels = depth_count.bit_length() - 1
    place = lax.axis_index("depth")
    piece = state
    for level in range(levels):
        half = piece.shape[1] // 2
        lower = piece[:, :half]
        upper = piece[:, half:]
        behind = place >> level & 1 == 1
        mine = jnp.where(behind, upper, lower)
        sent = jnp.where(behind, lower, upper)
        other = from_partner(sent, "depth", level)
        front = jnp.where(behind, other, mine)
        back = jnp.where(behind, mine, other)
        piece = composite(front, back)
    gathered = lax.all_gather(piece, "depth", axis=1, tiled=True)
    piece_len = pixels // depth_count
    split = gathered.reshape((4,) + (2,) * levels + (piece_len,))
    order = (0,) + tuple(range(levels, 0, -1)) + (levels + 1,)
    gathered = split.transpose(order).reshape(4, pixels)
    picture = gathered.reshape(4, rows, width)
    return jnp.concatenate([picture[:3], 1.0 - picture[3:4]], axis=0)


def solution(mesh):
    placed = (
        P("tile", "depth", None),
        P("tile", "depth", None),
        P("tile", "depth", None),
        P(),
        P(),
        P(),
    )
    return jax.shard_map(
        shards, mesh=mesh, in_specs=placed, out_specs=P(None, "tile", None), check_vma=False
    )
```

profile of v0, /device:TPU:8, one launch (start us, length us, event | category | flops | bytes accessed | tf_op | source)
XLA Modules:
  0.0 330.9 jit_solution(13423348183679817006)
XLA Ops:
  3.6 3.6 %collective-permute-start.1 = (f32[1,32,2048]{2,0,1:T(1,128)S(1)}, f32[1,32,2048]{2,0,1:T(1,128)S(1)}, u32[]{:S(2)}, u32[]{:S(2)}) collective-permute-start(f32[1,32,2048]{2,0,1:T(1,128)S(1)} %copy.14), channel_id=1, source_target_pairs={{64,0},{128,64},{192,128},{256,192},{320,256},{384,320},{448,384},... | collective-permute-start | bytes 786440 | tf_op jit(solution)/shard_map/ppermute | solution.py:15
  7.2 6.7 %copy.15 = f32[16,32,2048]{2,0,1:T(8,128)} copy(f32[16,32,2048]{2,1,0:T(8,128)} %param.8) | data formatting | bytes 8388608 | tf_op args[0]
  14.0 6.2 %pad_maximum_fusion = f32[18,32,2048]{2,0,1:T(8,128)} fusion(f32[1,32,2048]{2,0,1:T(1,128)S(1)} %collective-permute-done.1, f32[16,32,2048]{2,0,1:T(8,128)} %copy.15, f32[1,32,2048]{2,0,1:T(1,128)S(1)} %collective-permute-done), kind=kLoop, calls=%fused_computation.22 | loop fusion | flops 2359296 | bytes 9437184 | tf_op jit(solution)/shard_map/concatenate | solution.py:16
  20.1 140.3 %while.18 = (s32[]{:T(128)}, f32[3,16,2048]{2,1,0:T(8,128)S(1)}, f32[16,2048]{1,0:T(8,128)S(1)}, f32[1]{0:T(128)}, f32[18,32,2048]{2,0,1:T(8,128)}, /*index=5*/f...) while((s32[]{:T(128)}, f32[3,16,2048]{2,1,0:T(8,128)S(1)}, ...), condition=%wide.region_1.2_spmd.clone, body=%wide.region_0.1_spmd.clone.sunk | while | flops 1245189 | bytes 2363573 | solution.py:64
  21.9 2.5 fusion.38
  26.2 2.5 fusion.38
  30.6 2.5 fusion.38
  35.0 2.5 fusion.38
  39.4 2.5 fusion.38
  43.8 2.5 fusion.38
  48.2 2.5 fusion.38
  52.6 2.5 fusion.38
  87.6 2.5 fusion.38
  96.4 2.5 fusion.38
  161.1 3.8 %collective-permute-start.2 = (f32[4,16384]{1,0:T(4,128)S(1)}, f32[4,16384]{1,0:T(4,128)S(1)}, u32[]{:S(2)}, u32[]{:S(2)}) collective-permute-start(f32[4,16384]{1,0:T(4,128)S(1)} %get-tuple-element.294), channel_id=1, source_target_pairs={{0,1},{1,0},{2,3},{3,2},{4,5},{5,4},{6,7},{7,6},{8,9},{9,8},{10,11... | collective-permute-start | bytes 786440 | tf_op jit(solution)/shard_map/ppermute | solution.py:23
  165.0 6.4 %collective-permute-done.2 = f32[4,16384]{1,0:T(4,128)S(1)} collective-permute-done((f32[4,16384]{1,0:T(4,128)S(1)}, f32[4,16384]{1,0:T(4,128)S(1)}, u32[]{:S(2)}, u32[]{:S(2)}) %collective-permute-start.2) | collective-permute-done | bytes 262176 | tf_op jit(solution)/shard_map/ppermute | solution.py:23
  172.0 5.2 %collective-permute-start.3 = (f32[4,8192]{1,0:T(4,128)S(1)}, f32[4,8192]{1,0:T(4,128)S(1)}, u32[]{:S(2)}, u32[]{:S(2)}) collective-permute-start(f32[4,8192]{1,0:T(4,128)S(1)} %get-tuple-element.292), channel_id=1, source_target_pairs={{0,2},{1,3},{2,0},{3,1},{4,6},{5,7},{6,4},{7,5},{8,10},{9,11},{10,... | collective-permute-start | bytes 393224 | tf_op jit(solution)/shard_map/ppermute | solution.py:23
  177.2 5.8 %collective-permute-done.3 = f32[4,8192]{1,0:T(4,128)S(1)} collective-permute-done((f32[4,8192]{1,0:T(4,128)S(1)}, f32[4,8192]{1,0:T(4,128)S(1)}, u32[]{:S(2)}, u32[]{:S(2)}) %collective-permute-start.3) | collective-permute-done | bytes 131104 | tf_op jit(solution)/shard_map/ppermute | solution.py:23
  183.2 9.1 %collective-permute-start.4 = (f32[4,4096]{1,0:T(4,128)S(1)}, f32[4,4096]{1,0:T(4,128)S(1)}, u32[]{:S(2)}, u32[]{:S(2)}) collective-permute-start(f32[4,4096]{1,0:T(4,128)S(1)} %get-tuple-element.290), channel_id=1, source_target_pairs={{0,4},{1,5},{2,6},{3,7},{4,0},{5,1},{6,2},{7,3},{8,12},{9,13},{10,... | collective-permute-start | bytes 196616 | tf_op jit(solution)/shard_map/ppermute | solution.py:23
  192.3 3.7 %collective-permute-done.4 = f32[4,4096]{1,0:T(4,128)S(1)} collective-permute-done((f32[4,4096]{1,0:T(4,128)S(1)}, f32[4,4096]{1,0:T(4,128)S(1)}, u32[]{:S(2)}, u32[]{:S(2)}) %collective-permute-start.4) | collective-permute-done | bytes 65568 | tf_op jit(solution)/shard_map/ppermute | solution.py:23
  196.2 14.0 %collective-permute-start.5 = (f32[4,2048]{1,0:T(4,128)S(1)}, f32[4,2048]{1,0:T(4,128)S(1)}, u32[]{:S(2)}, u32[]{:S(2)}) collective-permute-start(f32[4,2048]{1,0:T(4,128)S(1)} %get-tuple-element.288), channel_id=1, source_target_pairs={{0,8},{1,9},{2,10},{3,11},{4,12},{5,13},{6,14},{7,15},{8,0},{9,1},... | collective-permute-start | bytes 98312 | tf_op jit(solution)/shard_map/ppermute | solution.py:23
  212.2 3.4 %collective-permute-start.6 = (f32[4,1024]{1,0:T(4,128)S(1)}, f32[4,1024]{1,0:T(4,128)S(1)}, u32[]{:S(2)}, u32[]{:S(2)}) collective-permute-start(f32[4,1024]{1,0:T(4,128)S(1)} %get-tuple-element.286), channel_id=1, source_target_pairs={{0,16},{1,17},{2,18},{3,19},{4,20},{5,21},{6,22},{7,23},{8,24},{9,... | collective-permute-start | bytes 49160 | tf_op jit(solution)/shard_map/ppermute | solution.py:23
  217.9 4.9 %collective-permute-start.7 = (f32[4,512]{1,0:T(4,128)S(1)}, f32[4,512]{1,0:T(4,128)S(1)}, u32[]{:S(2)}, u32[]{:S(2)}) collective-permute-start(f32[4,512]{1,0:T(4,128)S(1)} %get-tuple-element.284), channel_id=1, source_target_pairs={{0,32},{1,33},{2,34},{3,35},{4,36},{5,37},{6,38},{7,39},{8,40},{9,... | collective-permute-start | bytes 24584 | tf_op jit(solution)/shard_map/ppermute | solution.py:23
  225.0 103.5 %all_gather.3 = f32[4,32768]{1,0:T(4,128)S(1)} all-gather(f32[4,512]{1,0:T(4,128)S(1)} %pad_maximum_fusion.8), channel_id=1, replica_groups=mesh['tile'=8,'depth'=64] {'depth'}, dimensions={1}, use_global_device_ids=true | all-gather | bytes 532480 | tf_op jit(solution)/shard_map/all_gather | solution.py:81
  (171 shorter events, 127.9 us)
Async XLA Ops:
  0.0 13.9 %copy-start.2 = (s32[2,1,16]{2,1,0:T(1,128)S(1)}, s32[2,1,16]{2,1,0:T(1,128)}, u32[]{:S(2)}) copy-start(s32[2,1,16]{2,1,0:T(1,128)} %param.10) | copy-start | bytes 388
  0.0 13.9 %copy-start = (s32[2,1,16]{2,1,0:T(1,128)S(1)}, s32[2,1,16]{2,1,0:T(1,128)}, u32[]{:S(2)}) copy-start(s32[2,1,16]{2,1,0:T(1,128)} %param.9) | copy-start | bytes 388
  1.4 12.6 %collective-permute-start = (f32[1,32,2048]{2,0,1:T(1,128)S(1)}, f32[1,32,2048]{2,0,1:T(1,128)S(1)}, u32[]{:S(2)}, u32[]{:S(2)}) collective-permute-start(f32[1,32,2048]{2,0,1:T(1,128)S(1)} %copy.13), channel_id=1, source_target_pairs={{0,64},{64,128},{128,192},{192,256},{256,320},{320,384},{384,448},... | collective-permute-start | bytes 786440 | tf_op jit(solution)/shard_map/ppermute | solution.py:14
  3.6 10.4 %collective-permute-start.1 = (f32[1,32,2048]{2,0,1:T(1,128)S(1)}, f32[1,32,2048]{2,0,1:T(1,128)S(1)}, u32[]{:S(2)}, u32[]{:S(2)}) collective-permute-start(f32[1,32,2048]{2,0,1:T(1,128)S(1)} %copy.14), channel_id=1, source_target_pairs={{64,0},{128,64},{192,128},{256,192},{320,256},{384,320},{448,384},... | collective-permute-start | bytes 786440 | tf_op jit(solution)/shard_map/ppermute | solution.py:15
  13.9 6.2 %copy-start.1 = (f32[3]{0:T(128)S(1)}, f32[3]{0:T(128)}, u32[]{:S(2)}) copy-start(f32[3]{0:T(128)} %param.11) | copy-start | bytes 40
  161.1 10.2 %collective-permute-start.2 = (f32[4,16384]{1,0:T(4,128)S(1)}, f32[4,16384]{1,0:T(4,128)S(1)}, u32[]{:S(2)}, u32[]{:S(2)}) collective-permute-start(f32[4,16384]{1,0:T(4,128)S(1)} %get-tuple-element.294), channel_id=1, source_target_pairs={{0,1},{1,0},{2,3},{3,2},{4,5},{5,4},{6,7},{7,6},{8,9},{9,8},{10,11... | collective-permute-start | bytes 786440 | tf_op jit(solution)/shard_map/ppermute | solution.py:23
  172.0 11.0 %collective-permute-start.3 = (f32[4,8192]{1,0:T(4,128)S(1)}, f32[4,8192]{1,0:T(4,128)S(1)}, u32[]{:S(2)}, u32[]{:S(2)}) collective-permute-start(f32[4,8192]{1,0:T(4,128)S(1)} %get-tuple-element.292), channel_id=1, source_target_pairs={{0,2},{1,3},{2,0},{3,1},{4,6},{5,7},{6,4},{7,5},{8,10},{9,11},{10,... | collective-permute-start | bytes 393224 | tf_op jit(solution)/shard_map/ppermute | solution.py:23
  183.2 12.8 %collective-permute-start.4 = (f32[4,4096]{1,0:T(4,128)S(1)}, f32[4,4096]{1,0:T(4,128)S(1)}, u32[]{:S(2)}, u32[]{:S(2)}) collective-permute-start(f32[4,4096]{1,0:T(4,128)S(1)} %get-tuple-element.290), channel_id=1, source_target_pairs={{0,4},{1,5},{2,6},{3,7},{4,0},{5,1},{6,2},{7,3},{8,12},{9,13},{10,... | collective-permute-start | bytes 196616 | tf_op jit(solution)/shard_map/ppermute | solution.py:23
  196.2 15.9 %collective-permute-start.5 = (f32[4,2048]{1,0:T(4,128)S(1)}, f32[4,2048]{1,0:T(4,128)S(1)}, u32[]{:S(2)}, u32[]{:S(2)}) collective-permute-start(f32[4,2048]{1,0:T(4,128)S(1)} %get-tuple-element.288), channel_id=1, source_target_pairs={{0,8},{1,9},{2,10},{3,11},{4,12},{5,13},{6,14},{7,15},{8,0},{9,1},... | collective-permute-start | bytes 98312 | tf_op jit(solution)/shard_map/ppermute | solution.py:23
  212.2 5.6 %collective-permute-start.6 = (f32[4,1024]{1,0:T(4,128)S(1)}, f32[4,1024]{1,0:T(4,128)S(1)}, u32[]{:S(2)}, u32[]{:S(2)}) collective-permute-start(f32[4,1024]{1,0:T(4,128)S(1)} %get-tuple-element.286), channel_id=1, source_target_pairs={{0,16},{1,17},{2,18},{3,19},{4,20},{5,21},{6,22},{7,23},{8,24},{9,... | collective-permute-start | bytes 49160 | tf_op jit(solution)/shard_map/ppermute | solution.py:23
  217.9 7.0 %collective-permute-start.7 = (f32[4,512]{1,0:T(4,128)S(1)}, f32[4,512]{1,0:T(4,128)S(1)}, u32[]{:S(2)}, u32[]{:S(2)}) collective-permute-start(f32[4,512]{1,0:T(4,128)S(1)} %get-tuple-element.284), channel_id=1, source_target_pairs={{0,32},{1,33},{2,34},{3,35},{4,36},{5,37},{6,38},{7,39},{8,40},{9,... | collective-permute-start | bytes 24584 | tf_op jit(solution)/shard_map/ppermute | solution.py:23
where the time goes:
time: 334 us; the launch traced here: 331 us
  other arithmetic  147 us (44%)
  blocking collectives  103 us (31%)
  starting transfers between devices  46 us (14%)
  waiting for transfers between devices  22 us (7%)
  local copies, waits for them, and re-layouts  10.5 us (3%)
    all_gather x1, blocking collectives, shards(): gathered = lax.all_gather(piece, 'depth', axis=1, tiled=True)  103 us
    mul x32, other arithmetic, march(): weight = trans * (1.0 - keep) * source  80.2 us
    mul x32, other arithmetic, march(): return (color, trans * keep)  55.1 us
    ppermute x6, starting transfers between devices, from_partner(): return lax.ppermute(value, axis, pairs)  40.5 us
    ppermute x6, waiting for transfers between devices, from_partner(): return lax.ppermute(value, axis, pairs)  22 us
    unnamed x9, local copies, waits for them, and re-layouts  7.1 us
  transfers between devices with their start and end apart: 8, of which 6 were waited for; matrix products, arithmetic and copies ran while one was open for 2% of the time, Pallas kernels for 0%

commit v1 on v0

v1 whole, which is shorter than its diff:
```python
import functools
import math

import jax
import jax.numpy as jnp
from jax import lax
from jax.experimental import pallas as pl
from jax.experimental.pallas import tpu as pltpu
from jax.sharding import PartitionSpec as P

MESH = pl.DeviceIdType.MESH
BR, BW = 8, 128


def render(
    nt, nx, nz, density, start, count, emission, extinction, edge_gain, image,
    field, states, parts, mixed, crossed, pieces,
    load_sem, halo_send, halo_recv, z_send, z_recv, x_send, x_recv, g_send, g_recv, f_send, f_recv,
):
    rows, slices, width = density.shape
    blocks = width // BW
    bricks = rows // BR
    tile = lax.axis_index("tile")
    place = lax.axis_index("depth")
    x, z = place // nz, lax.rem(place, nz)

    def at(px, pz):
        return (tile, px * nz + pz)

    barrier = pltpu.get_barrier_semaphore()

    def greet_z(j, _):
        pl.semaphore_signal(barrier, inc=1, device_id=at(x, lax.rem(z + j, nz)), device_id_type=MESH)
        return 0

    def greet_x(j, _):
        pl.semaphore_signal(barrier, inc=1, device_id=at(lax.rem(x + j, nx), z), device_id_type=MESH)
        return 0

    above = lax.rem(tile + nt - 1, nt)
    below = lax.rem(tile + 1, nt)
    pl.semaphore_signal(barrier, inc=1, device_id=(above, place), device_id_type=MESH)
    pl.semaphore_signal(barrier, inc=1, device_id=(below, place), device_id_type=MESH)
    lax.fori_loop(1, nz, greet_z, 0)
    lax.fori_loop(1, nx, greet_x, 0)

    def load(b):
        return pltpu.make_async_copy(
            density.at[:, :, pl.ds(pl.multiple_of(b * BW, BW), BW)],
            field.at[b + 1, pl.ds(1, rows)],
            load_sem.at[b],
        )

    def start_load(b, _):
        load(b).start()
        return 0

    lax.fori_loop(0, blocks, start_load, 0)
    zeros = jnp.zeros((rows + 2, slices, BW), jnp.float32)
    field[0] = zeros
    field[blocks + 1] = zeros

    def turn(i):
        gap = (blocks // 2) - (i + 1) // 2
        side = jnp.where(lax.rem(i, 2) == 1, blocks - gap, gap)
        return lax.rem(z + side, blocks)

    pl.semaphore_wait(barrier, nz - 1 + nx - 1 + 2)

    def halo_up(b):
        return pltpu.make_async_remote_copy(
            density.at[0, :, pl.ds(pl.multiple_of(b * BW, BW), BW)],
            field.at[b + 1, rows + 1],
            halo_send.at[0, b],
            halo_recv.at[0, b],
            device_id=(above, place),
            device_id_type=MESH,
        )

    def halo_down(b):
        return pltpu.make_async_remote_copy(
            density.at[rows - 1, :, pl.ds(pl.multiple_of(b * BW, BW), BW)],
            field.at[b + 1, 0],
            halo_send.at[1, b],
            halo_recv.at[1, b],
            device_id=(below, place),
            device_id_type=MESH,
        )

    def start_halo(i, _):
        b = turn(i)
        halo_up(b).start()
        halo_down(b).start()
        return 0

    lax.fori_loop(0, blocks, start_halo, 0)

    def end_load(b, _):
        load(b).wait()
        return 0

    lax.fori_loop(0, blocks, end_load, 0)

    lane = lax.broadcasted_iota(jnp.int32, (BR, BW), 1)
    first_lane, last_lane = lane == 0, lane == BW - 1
    sub = lax.broadcasted_iota(jnp.int32, (BR, BW), 0)
    rate = extinction[0] * (-math.log2(math.e) / (slices * nx * nz))
    gain = edge_gain[0] * 0.25
    top = jnp.where(tile == 0, 0.0, 1.0)
    bottom = jnp.where(tile == nt - 1, 0.0, 1.0)
    weight_up = jnp.where(sub == 0, top, 1.0)
    weight_down = jnp.where(sub == BR - 1, bottom, 1.0)

    def march(b):
        flat = [field.at[b + j].reshape((rows + 2) * slices, BW) for j in range(3)]

        def step(k, carry):
            out = []
            for h in range(bricks):
                total, trans, color = carry[h]
                base = (BR * h + 1) * slices + k
                left, mid, right = (f[pl.ds(base, BR, stride=slices)] for f in flat)
                up = flat[1][pl.ds(base - slices, BR, stride=slices)]
                down = flat[1][pl.ds(base + slices, BR, stride=slices)]
                if h == 0:
                    up = up * weight_up
                if h == bricks - 1:
                    down = down * weight_down
                before = pltpu.roll(jnp.where(last_lane, left, mid), 1, 1)
                after = pltpu.roll(jnp.where(first_lane, right, mid), BW - 1, 1)
                grad_y, grad_x = down - up, after - before
                source = mid + gain * (grad_y * grad_y + grad_x * grad_x)
                low = start[h, 0, b]
                live = jnp.logical_and(low <= k, k < low + count[h, 0, b])
                total = total + jnp.where(live, rate, 0.0) * mid
                later = jnp.exp2(total)
                out.append((total, later, color + (trans - later) * source))
            return tuple(out)

        zero, one = jnp.zeros((BR, BW), jnp.float32), jnp.ones((BR, BW), jnp.float32)
        done = lax.fori_loop(0, slices, step, ((zero, one, zero),) * bricks, unroll=8)
        return [(color, trans) for _, trans, color in done]

    def z_copy(b):
        return pltpu.make_async_remote_copy(
            states.at[b], parts.at[z], z_send.at[b], z_recv.at[z], device_id=at(x, b), device_id_type=MESH
        )

    def one_block(i, _):
        b = turn(i)
        halo_up(b).wait_recv()
        halo_down(b).wait_recv()
        for h, (color, trans) in enumerate(march(b)):
            states[b, 2 * h] = color
            states[b, 2 * h + 1] = trans

        @pl.when(i < blocks - 1)
        def _():
            z_copy(b).start()

        return 0

    lax.fori_loop(0, blocks, one_block, 0)
    parts[z] = states[z]

    def arrived(j, _):
        @pl.when(j != z)
        def _():
            pltpu.make_async_remote_copy(
                states.at[j], parts.at[j], z_send.at[j], z_recv.at[j], device_id=at(x, j), device_id_type=MESH
            ).wait_recv()

        return 0

    lax.fori_loop(0, nz, arrived, 0)

    def over(j, carry):
        out = []
        for h in range(bricks):
            color, trans = carry[h]
            out.append((color + trans * parts[j, 2 * h], trans * parts[j, 2 * h + 1]))
        return tuple(out)

    zero, one = jnp.zeros((BR, BW), jnp.float32), jnp.ones((BR, BW), jnp.float32)
    merged = lax.fori_loop(0, nz, over, ((zero, one),) * bricks)

    half = BR // 2
    upper = sub < half
    for h, (color, trans) in enumerate(merged):
        mixed[2 * h] = jnp.where(upper, color, pltpu.roll(trans, half, 0))
        mixed[2 * h + 1] = jnp.where(upper, pltpu.roll(color, half, 0), trans)

    def x_copy(j):
        other = lax.rem(x + j, nx)
        return pltpu.make_async_remote_copy(
            mixed.at[other], crossed.at[x], x_send.at[j], x_recv.at[x], device_id=at(other, z), device_id_type=MESH
        )

    for j in range(1, nx):
        x_copy(j).start()
    crossed[x] = mixed[x]
    for j in range(1, nx):
        other = lax.rem(x + j, nx)
        pltpu.make_async_remote_copy(
            mixed.at[x], crossed.at[other], x_send.at[j], x_recv.at[other], device_id=at(other, z), device_id_type=MESH
        ).wait_recv()
    final = crossed[0]
    for j in range(1, nx):
        nearer = jnp.where(upper, pltpu.roll(final, half, 0), final)
        final = jnp.where(upper, final, 0.0) + nearer * crossed[j]
    pieces[x, z] = final

    def g_copy(j):
        return pltpu.make_async_remote_copy(
            pieces.at[x, z], pieces.at[x, z], g_send.at[j], g_recv.at[z],
            device_id=at(x, lax.rem(z + j, nz)), device_id_type=MESH,
        )

    def start_g(j, _):
        g_copy(j).start()
        return 0

    lax.fori_loop(1, nz, start_g, 0)

    def wait_g(j, _):
        other = lax.rem(z + j, nz)
        pltpu.make_async_remote_copy(
            pieces.at[x, other], pieces.at[x, other], g_send.at[j], g_recv.at[other],
            device_id=at(x, other), device_id_type=MESH,
        ).wait_recv()
        return 0

    lax.fori_loop(1, nz, wait_g, 0)

    def f_copy(j):
        return pltpu.make_async_remote_copy(
            pieces.at[x], pieces.at[x], f_send.at[j], f_recv.at[x],
            device_id=at(lax.rem(x + j, nx), z), device_id_type=MESH,
        )

    for j in range(1, nx):
        f_copy(j).start()
    for j in range(1, nx):
        other = lax.rem(x + j, nx)
        pltpu.make_async_remote_copy(
            pieces.at[other], pieces.at[other], f_send.at[j], f_recv.at[other],
            device_id=at(other, z), device_id_type=MESH,
        ).wait_recv()

    for b in range(blocks):
        for h in range(bricks):
            first, second = pieces[2 * h, b], pieces[2 * h + 1, b]
            color = jnp.where(upper, first, pltpu.roll(second, half, 0))
            trans = jnp.where(upper, pltpu.roll(first, half, 0), second)
            spot = (pl.ds(BR * h, BR), pl.ds(BW * b, BW))
            for c in range(3):
                image[(c,) + spot] = emission[c] * color
            image[(3,) + spot] = 1.0 - trans

    def end_halo(b, _):
        halo_up(b).wait_send()
        halo_down(b).wait_send()
        return 0

    def end_z(j, _):
        z_copy(lax.rem(z + j, nz)).wait_send()
        g_copy(j).wait_send()
        return 0

    lax.fori_loop(0, blocks, end_halo, 0)
    lax.fori_loop(1, nz, end_z, 0)
    for j in range(1, nx):
        x_copy(j).wait_send()
        f_copy(j).wait_send()


def shards(nt, nx, nz, density, slab_start, slab_count, emission, extinction, edge_gain):
    rows, slices, width = density.shape
    blocks, bricks = width // BW, rows // BR
    vmem, smem, anywhere = (pl.BlockSpec(memory_space=m) for m in (pltpu.VMEM, pltpu.SMEM, pl.ANY))
    dma = pltpu.SemaphoreType.DMA
    return pl.pallas_call(
        functools.partial(render, nt, nx, nz),
        out_shape=jax.ShapeDtypeStruct((4, rows, width), jnp.float32),
        in_specs=[anywhere] + [smem] * 5,
        out_specs=vmem,
        scratch_shapes=[
            pltpu.VMEM((blocks + 2, rows + 2, slices, BW), jnp.float32),
            pltpu.VMEM((blocks, 2 * bricks, BR, BW), jnp.float32),
            pltpu.VMEM((nz, 2 * bricks, BR, BW), jnp.float32),
            pltpu.VMEM((nx, BR, BW), jnp.float32),
            pltpu.VMEM((nx, BR, BW), jnp.float32),
            pltpu.VMEM((nx, nz, BR, BW), jnp.float32),
            dma((blocks,)),
            dma((2, blocks)),
            dma((2, blocks)),
            dma((blocks,)),
            dma((nz,)),
            dma((nx,)),
            dma((nx,)),
            dma((nz,)),
            dma((nz,)),
            dma((nx,)),
            dma((nx,)),
        ],
        compiler_params=pltpu.CompilerParams(
            collective_id=0, has_side_effects=True, vmem_limit_bytes=32 * 1024 * 1024
        ),
        name="render",
    )(density, slab_start, slab_count, emission, extinction, edge_gain)


def solution(mesh):
    placed = (
        P("tile", "depth", None),
        P("tile", "depth", None),
        P("tile", "depth", None),
        P(),
        P(),
        P(),
    )
    nt, nd = mesh.shape["tile"], mesh.shape["depth"]
    nz = 16
    return jax.shard_map(
        functools.partial(shards, nt, nd // nz, nz),
        mesh=mesh,
        in_specs=placed,
        out_specs=P(None, "tile", None),
        check_vma=False,
    )
```

time: 334 us -> 58.7 us (0.18)
  the two profiles are of different devices: /device:TPU:8 before, /device:TPU:4 now
where the time goes in v1:
time: 58.7 us; the launch traced here: 58.5 us
  Pallas kernels  52.2 us (89%)
  local copies, waits for them, and re-layouts  4.99 us (9%)
  between operations  1.32 us (2%)
    pallas_call x1, Pallas kernels, shards(): pl.pallas_call(functools.partial(render, nt, nx, nz), out_shape=jax.Shape...  52.2 us
    unnamed x9, local copies, waits for them, and re-layouts  4.99 us

profile of v1, /device:TPU:4, one launch (start us, length us, event | category | flops | bytes accessed | tf_op | source)
XLA Modules:
  0.0 58.5 jit_solution(6635202545534023884)
XLA Ops:
  1.3 0.0 copy-start
  1.3 2.2 %copy-done = f32[16,32,2048]{2,1,0:T(8,128)S(1)} copy-done((f32[16,32,2048]{2,1,0:T(8,128)S(1)}, f32[16,32,2048]{2,1,0:T(8,128)}, u32[]{:S(2)}) %copy-start) | copy-done | bytes 4194328
  3.5 0.0 copy-start.1
  3.5 0.7 %copy-done.1 = s32[2,1,16]{2,1,0:T(1,128)S(1)} copy-done((s32[2,1,16]{2,1,0:T(1,128)S(1)}, s32[2,1,16]{2,1,0:T(1,128)}, u32[]{:S(2)}) %copy-start.1) | copy-done | bytes 152
  4.2 0.0 copy-start.2
  4.2 0.7 %copy-done.2 = s32[2,1,16]{2,1,0:T(1,128)S(1)} copy-done((s32[2,1,16]{2,1,0:T(1,128)S(1)}, s32[2,1,16]{2,1,0:T(1,128)}, u32[]{:S(2)}) %copy-start.2) | copy-done | bytes 152
  4.8 0.0 copy-start.3
  4.8 0.7 %copy-done.3 = f32[3]{0:T(128)S(1)} copy-done((f32[3]{0:T(128)S(1)}, f32[3]{0:T(128)}, u32[]{:S(2)}) %copy-start.3) | copy-done | bytes 36
  5.5 52.2 %render.1 = f32[4,16,2048]{2,1,0:T(8,128)S(1)} custom-call(f32[16,32,2048]{2,1,0:T(8,128)S(1)} %copy-done, s32[2,1,16]{2,1,0:T(1,128)S(1)} %copy-done.1, s32[2,1,16]{2,1,0:T(1,128)S(1)} %copy-done.2, f32[3]{0:T(128)S(1)} %copy-done.3, f32[1]{0:T(128)S(6)} %copy.8.extinction, f32[1]{0:T(128)S(6)} %copy.9.edge_gain), custom_call_target="tpu_custom_call" | custom-call | tf_op jit(solution)/shard_map/render/pallas_call | solution.py:282
  57.7 0.8 %copy.10 = f32[4,16,2048]{2,1,0:T(8,128)} copy(f32[4,16,2048]{2,1,0:T(8,128)S(1)} %render.1) | data formatting | bytes 1048576
Async XLA Ops:
  1.3 2.2 %copy-start = (f32[16,32,2048]{2,1,0:T(8,128)S(1)}, f32[16,32,2048]{2,1,0:T(8,128)}, u32[]{:S(2)}) copy-start(f32[16,32,2048]{2,1,0:T(8,128)} %density.1) | copy-start | bytes 12582916
  3.5 0.7 %copy-start.1 = (s32[2,1,16]{2,1,0:T(1,128)S(1)}, s32[2,1,16]{2,1,0:T(1,128)}, u32[]{:S(2)}) copy-start(s32[2,1,16]{2,1,0:T(1,128)} %start.1) | copy-start | bytes 388
  4.2 0.7 %copy-start.2 = (s32[2,1,16]{2,1,0:T(1,128)S(1)}, s32[2,1,16]{2,1,0:T(1,128)}, u32[]{:S(2)}) copy-start(s32[2,1,16]{2,1,0:T(1,128)} %count.1) | copy-start | bytes 388
  4.8 0.7 %copy-start.3 = (f32[3]{0:T(128)S(1)}, f32[3]{0:T(128)}, u32[]{:S(2)}) copy-start(f32[3]{0:T(128)} %emission.1) | copy-start | bytes 40

commit v2 on v1

v2 whole, which is shorter than its diff:
```python
import functools
import math

import jax
import jax.numpy as jnp
from jax import lax
from jax.experimental import pallas as pl
from jax.experimental.pallas import tpu as pltpu
from jax.sharding import PartitionSpec as P

MESH = pl.DeviceIdType.MESH
BR, BW = 8, 128
HALF = BR // 2
PAD = 8
NEAR = 4


def render(
    nt, nx, nz, density, start_in, count_in, emission_in, extinction_in, edge_gain_in, image,
    start, count, emission, extinction, edge_gain, field, states, parts, pieces,
    small_sem, load_sem, halo_send, halo_recv, near_sem, far_sem, r_send, r_recv, g_send, g_recv, f_send, f_recv, o_sem,
):
    rows, slices, width = density.shape
    blocks = width // BW
    bricks = rows // BR
    tile = lax.axis_index("tile")
    place = lax.axis_index("depth")
    x, z = place // nz, lax.rem(place, nz)
    has_above, has_below = tile > 0, tile < nt - 1
    above, below = jnp.where(has_above, tile - 1, tile + 1), jnp.where(has_below, tile + 1, tile - 1)

    def at(px, pz):
        return (tile, px * nz + pz)

    def along(dz):
        return lax.rem(z + dz + nz, nz)

    barrier = pltpu.get_barrier_semaphore()
    reach = NEAR // 2

    @pl.when(has_above)
    def _():
        pl.semaphore_signal(barrier, inc=1, device_id=(above, place), device_id_type=MESH)

    @pl.when(has_below)
    def _():
        pl.semaphore_signal(barrier, inc=1, device_id=(below, place), device_id_type=MESH)

    for dz in range(-reach, reach + 1):
        for dx in range(nx):
            if dx or dz:
                pl.semaphore_signal(
                    barrier, inc=1, device_id=at(lax.rem(x + dx, nx), along(dz)), device_id_type=MESH
                )

    small = [
        pltpu.make_async_copy(source, target, small_sem.at[i])
        for i, (source, target) in enumerate((
            (start_in, start), (count_in, count), (emission_in, emission),
            (extinction_in, extinction), (edge_gain_in, edge_gain),
        ))
    ]
    for copy in small:
        copy.start()

    def load(b):
        return pltpu.make_async_copy(
            density.at[:, :, pl.ds(pl.multiple_of(b * BW, BW), BW)],
            field.at[b + 1, pl.ds(1, rows), pl.ds(0, slices)],
            load_sem.at[b],
        )

    def start_load(b, _):
        load(b).start()
        return 0

    lax.fori_loop(0, blocks, start_load, 0)
    zeros = jnp.zeros((rows + 2, slices + PAD, BW), jnp.float32)
    field[0] = zeros
    field[blocks + 1] = zeros
    edge = jnp.zeros((blocks, slices, BW), jnp.float32)

    @pl.when(jnp.logical_not(has_above))
    def _():
        field[pl.ds(1, blocks), 0, pl.ds(0, slices)] = edge

    @pl.when(jnp.logical_not(has_below))
    def _():
        field[pl.ds(1, blocks), rows + 1, pl.ds(0, slices)] = edge


    def turn(i):
        gap = jnp.where(i < 2 * NEAR, NEAR - i // 2, 2 * NEAR - (i - 2 * NEAR + 1) // 2)
        gap = jnp.where(i == blocks - 1, 0, gap)
        return lax.rem(z + jnp.where(lax.rem(i, 2) == 1, nz - gap, gap), nz)

    def halo_up(b):
        return pltpu.make_async_remote_copy(
            density.at[0, :, pl.ds(pl.multiple_of(b * BW, BW), BW)],
            field.at[b + 1, rows + 1, pl.ds(0, slices)],
            halo_send.at[0, b],
            halo_recv.at[0, b],
            device_id=(above, place),
            device_id_type=MESH,
        )

    def halo_down(b):
        return pltpu.make_async_remote_copy(
            density.at[rows - 1, :, pl.ds(pl.multiple_of(b * BW, BW), BW)],
            field.at[b + 1, 0, pl.ds(0, slices)],
            halo_send.at[1, b],
            halo_recv.at[1, b],
            device_id=(below, place),
            device_id_type=MESH,
        )

    def start_halo(i, _):
        b = turn(i)

        @pl.when(has_above)
        def _():
            halo_up(b).start()

        @pl.when(has_below)
        def _():
            halo_down(b).start()

        return 0

    pl.semaphore_wait(barrier, nx * (2 * reach + 1) + jnp.where(jnp.logical_and(has_above, has_below), 1, 0))
    for dz in (-reach, reach):
        pl.semaphore_signal(near_sem, inc=1, device_id=at(x, along(dz)), device_id_type=MESH)
    lax.fori_loop(0, blocks, start_halo, 0)
    pl.semaphore_wait(near_sem, 2)
    for dz in (-NEAR, NEAR):
        pl.semaphore_signal(far_sem, inc=1, device_id=at(x, along(dz)), device_id_type=MESH)

    def end_load(b, _):
        load(b).wait()
        return 0

    lax.fori_loop(0, blocks, end_load, 0)
    for copy in small:
        copy.wait()

    lane = lax.broadcasted_iota(jnp.int32, (BR, BW), 1)
    first_lane, last_lane = lane == 0, lane == BW - 1
    sub = lax.broadcasted_iota(jnp.int32, (BR, BW), 0)
    upper = sub < HALF
    rate = extinction[0] * (-math.log2(math.e) / (slices * nx * nz))
    gain = edge_gain[0] * 0.25
    zero, one = jnp.zeros((BR, BW), jnp.float32), jnp.ones((BR, BW), jnp.float32)

    def march(b):
        stride = slices + PAD
        flat = [field.at[b + j].reshape((rows + 2) * stride, BW) for j in range(3)]
        ranges = [(start[h, 0, b], start[h, 0, b] + count[h, 0, b]) for h in range(bricks)]

        def step(k, carry):
            result = []
            for h in range(bricks):
                total, trans, color = carry[h]
                base = (BR * h + 1) * stride + k
                left, mid, right = (f[pl.ds(base, BR, stride=stride)] for f in flat)
                up = flat[1][pl.ds(base - stride, BR, stride=stride)]
                down = flat[1][pl.ds(base + stride, BR, stride=stride)]
                before = pltpu.roll(jnp.where(last_lane, left, mid), 1, 1)
                after = pltpu.roll(jnp.where(first_lane, right, mid), BW - 1, 1)
                grad_y, grad_x = down - up, after - before
                source = mid + gain * (grad_y * grad_y + grad_x * grad_x)
                low, high = ranges[h]
                live = jnp.logical_and(low <= k, k < high)
                total = total + jnp.where(live, rate, 0.0) * mid
                later = jnp.exp2(total)
                result.append((total, later, color + (trans - later) * source))
            return tuple(result)

        done = lax.fori_loop(0, slices, step, ((zero, one, zero),) * bricks, unroll=slices)
        return [(color, trans) for _, trans, color in done]

    def r_copy(q, b):
        return pltpu.make_async_remote_copy(
            states.at[b, q], parts.at[place], r_send.at[b, q], r_recv, device_id=at(q, b), device_id_type=MESH
        )

    def one_block(i, _):
        b = turn(i)

        @pl.when(has_below)
        def _():
            halo_up(b).wait_recv()

        @pl.when(has_above)
        def _():
            halo_down(b).wait_recv()

        for h, (color, trans) in enumerate(march(b)):
            states[b, 2 * h] = jnp.where(upper, color, pltpu.roll(trans, HALF, 0))
            states[b, 2 * h + 1] = jnp.where(upper, pltpu.roll(color, HALF, 0), trans)
        return b

    def sent_block(i, _):
        b = one_block(i, 0)
        for q in range(nx):
            r_copy(q, b).start()
        return 0

    lax.fori_loop(0, 2 * NEAR, sent_block, 0)
    pl.semaphore_wait(far_sem, 2)
    lax.fori_loop(2 * NEAR, blocks - 1, sent_block, 0)
    one_block(blocks - 1, 0)
    for j in range(1, nx):
        r_copy(lax.rem(x + j, nx), z).start()
    parts[place] = states[z, x]

    others = pl.ds(0, nx * nz - 1)
    pltpu.make_async_remote_copy(
        parts.at[others], parts.at[others], o_sem, r_recv, device_id=at(lax.rem(x + 1, nx), z), device_id_type=MESH
    ).wait_recv()

    def over(j, carry):
        color, trans = carry
        part = parts[j]
        both = jnp.where(upper, pltpu.roll(part, HALF, 0), part)
        return color + trans * part, trans * both

    color, trans = lax.fori_loop(0, nx * nz, over, (zero, one), unroll=nz)
    pieces[x, z] = jnp.where(upper, color, trans)

    def g_copy(j):
        return pltpu.make_async_remote_copy(
            pieces.at[x, z], pieces.at[x, z], g_send.at[j], g_recv.at[z], device_id=at(x, lax.rem(z + j, nz)), device_id_type=MESH
        )

    def f_copy(j, other):
        return pltpu.make_async_remote_copy(
            pieces.at[x, other], pieces.at[x, other], f_send.at[j], f_recv.at[x],
            device_id=at(lax.rem(x + j, nx), z), device_id_type=MESH,
        )

    def arrive(i):
        gap = i // 2 + 1
        return jnp.where(lax.rem(i, 2) == 1, nz - gap, gap)

    def start_g(i, _):
        g_copy(arrive(nz - 2 - i)).start()
        return 0

    lax.fori_loop(0, nz - 1, start_g, 0)
    for j in range(1, nx):
        f_copy(j, z).start()

    def pass_on(i, _):
        other = lax.rem(z + arrive(i), nz)
        pltpu.make_async_remote_copy(
            pieces.at[x, other], pieces.at[x, other], g_send.at[other], g_recv.at[other],
            device_id=at(x, other), device_id_type=MESH,
        ).wait_recv()
        for j in range(1, nx):
            f_copy(j, other).start()
        return 0

    lax.fori_loop(0, nz - 1, pass_on, 0)

    def whole(j):
        other = lax.rem(x + j, nx)
        return pltpu.make_async_remote_copy(
            pieces.at[other], pieces.at[other], f_send.at[j], f_recv.at[other],
            device_id=at(other, z), device_id_type=MESH,
        )

    for j in range(1, nx):
        whole(j).wait_recv()

    for b in range(blocks):
        for h in range(bricks):
            first, second = pieces[2 * h, b], pieces[2 * h + 1, b]
            color = jnp.where(upper, first, pltpu.roll(second, HALF, 0))
            trans = jnp.where(upper, pltpu.roll(first, HALF, 0), second)
            spot = (pl.ds(BR * h, BR), pl.ds(BW * b, BW))
            for c in range(3):
                image[(c,) + spot] = emission[c] * color
            image[(3,) + spot] = 1.0 - trans

    def end_halo(b, _):
        @pl.when(has_above)
        def _():
            halo_up(b).wait_send()

        @pl.when(has_below)
        def _():
            halo_down(b).wait_send()

        for q in range(nx):
            @pl.when(jnp.logical_or(q != x, b != z))
            def _():
                r_copy(q, b).wait_send()
        return 0

    def end_g(j, _):
        g_copy(j).wait_send()
        return 0

    lax.fori_loop(0, blocks, end_halo, 0)
    lax.fori_loop(1, nz, end_g, 0)
    for j in range(1, nx):
        whole(j).wait_send()


def shards(nt, nx, nz, density, slab_start, slab_count, emission, extinction, edge_gain):
    rows, slices, width = density.shape
    blocks = width // BW
    hbm = pl.BlockSpec(memory_space=pltpu.HBM)
    dma, plain = pltpu.SemaphoreType.DMA, pltpu.SemaphoreType.REGULAR
    return pl.pallas_call(
        functools.partial(render, nt, nx, nz),
        out_shape=pltpu.VMEM((4, rows, width), jnp.float32),
        in_specs=[hbm] * 6,
        out_specs=pl.BlockSpec(memory_space=pltpu.VMEM),
        scratch_shapes=[
            pltpu.SMEM(slab_start.shape, jnp.int32),
            pltpu.SMEM(slab_count.shape, jnp.int32),
            pltpu.SMEM(emission.shape, jnp.float32),
            pltpu.SMEM(extinction.shape, jnp.float32),
            pltpu.SMEM(edge_gain.shape, jnp.float32),
            pltpu.VMEM((blocks + 2, rows + 2, slices + PAD, BW), jnp.float32),
            pltpu.VMEM((blocks, nx, BR, BW), jnp.float32),
            pltpu.VMEM((nx * nz, BR, BW), jnp.float32),
            pltpu.VMEM((nx, nz, BR, BW), jnp.float32),
            dma((5,)),
            dma((blocks,)),
            dma((2, blocks)),
            dma((2, blocks)),
            plain,
            plain,
            dma((blocks, nx)),
            dma,
            dma((nz,)),
            dma((nz,)),
            dma((nx,)),
            dma((nx,)),
            dma,
        ],
        compiler_params=pltpu.CompilerParams(
            collective_id=0, has_side_effects=True, vmem_limit_bytes=56 * 1024 * 1024
        ),
        name="render",
    )(density, slab_start, slab_count, emission, extinction, edge_gain)


def solution(mesh):
    placed = (
        P("tile", "depth", None),
        P("tile", "depth", None),
        P("tile", "depth", None),
        P(),
        P(),
        P(),
    )
    nt, nd = mesh.shape["tile"], mesh.shape["depth"]
    nz = 16
    return jax.shard_map(
        functools.partial(shards, nt, nd // nz, nz),
        mesh=mesh,
        in_specs=placed,
        out_specs=P(None, "tile", None),
        check_vma=False,
    )
```

time: 58.7 us -> 48.4 us (0.82)
  the two profiles are of different devices: /device:TPU:4 before, /device:TPU:1 now
where the time goes in v2:
time: 48.4 us; the launch traced here: 47.5 us
  Pallas kernels  45.4 us (94%)
  between operations  1.3 us (3%)
  local copies, waits for them, and re-layouts  0.8 us (2%)
    pallas_call x1, Pallas kernels, shards(): pl.pallas_call(functools.partial(render, nt, nx, nz), out_shape=pltpu.VME...  45.4 us

profile of v2, /device:TPU:1, one launch (start us, length us, event | category | flops | bytes accessed | tf_op | source)
XLA Modules:
  0.0 47.5 jit_solution(6193275932338698013)
XLA Ops:
  1.3 45.4 %render.1 = f32[4,16,2048]{2,1,0:T(8,128)S(1)} custom-call(f32[16,32,2048]{2,1,0:T(8,128)} %density.1, s32[2,1,16]{2,1,0:T(1,128)} %start_in.1, s32[2,1,16]{2,1,0:T(1,128)} %count_in.1, f32[3]{0:T(128)} %emission_in.1, f32[1]{0:T(128)S(6)} %copy.9.extinction_in, f32[1]{0:T(128)S(6)} %copy.10.edge_gain_in), custom_call_target="tpu_custom_call" | custom-call | tf_op jit(solution)/shard_map/render/pallas_call | solution.py:315
  46.8 0.8 %copy.8 = f32[4,16,2048]{2,1,0:T(8,128)} copy(f32[4,16,2048]{2,1,0:T(8,128)S(1)} %render.1) | data formatting | bytes 1048576

commit v3 on v2

--- a/solution.py
+++ b/solution.py
@@ -12,13 +12,13 @@
 BR, BW = 8, 128
 HALF = BR // 2
 PAD = 8
-NEAR = 4
+REACH = 2
 
 
 def render(
     nt, nx, nz, density, start_in, count_in, emission_in, extinction_in, edge_gain_in, image,
-    start, count, emission, extinction, edge_gain, field, states, parts, pieces,
-    small_sem, load_sem, halo_send, halo_recv, near_sem, far_sem, r_send, r_recv, g_send, g_recv, f_send, f_recv, o_sem,
+    start, count, emission, extinction, edge_gain, field, swap_out, swap_in, states, parts, pieces,
+    small_sem, load_sem, halo_send, halo_recv, heard, s_send, s_recv, r_send, r_recv, g_send, g_recv, f_send, f_recv, o_sem,
 ):
     rows, slices, width = density.shape
     blocks = width // BW
@@ -26,6 +26,9 @@
     tile = lax.axis_index("tile")
     place = lax.axis_index("depth")
     x, z = place // nz, lax.rem(place, nz)
+    groups = nz // 2
+    group, member = z // 2, lax.rem(z, 2)
+    partner = z + 1 - 2 * member
     has_above, has_below = tile > 0, tile < nt - 1
     above, below = jnp.where(has_above, tile - 1, tile + 1), jnp.where(has_below, tile + 1, tile - 1)
 
@@ -36,7 +39,6 @@
         return lax.rem(z + dz + nz, nz)
 
     barrier = pltpu.get_barrier_semaphore()
-    reach = NEAR // 2
 
     @pl.when(has_above)
     def _():
@@ -46,7 +48,7 @@
     def _():
         pl.semaphore_signal(barrier, inc=1, device_id=(below, place), device_id_type=MESH)
 
-    for dz in range(-reach, reach + 1):
+    for dz in range(-REACH, REACH + 1):
         for dx in range(nx):
             if dx or dz:
                 pl.semaphore_signal(
@@ -90,15 +92,17 @@
 
 
     def turn(i):
-        gap = jnp.where(i < 2 * NEAR, NEAR - i // 2, 2 * NEAR - (i - 2 * NEAR + 1) // 2)
-        gap = jnp.where(i == blocks - 1, 0, gap)
-        return lax.rem(z + jnp.where(lax.rem(i, 2) == 1, nz - gap, gap), nz)
+        gap = groups // 2 - (i + 1) // 2
+        return lax.rem(group + jnp.where(lax.rem(i, 2) == 1, gap, groups - gap), groups)
+
+    def block(i):
+        return 2 * turn(lax.rem(i, groups)) + jnp.where(i < groups, 1 - member, member)
 
     def halo_up(b):
         return pltpu.make_async_remote_copy(
             density.at[0, :, pl.ds(pl.multiple_of(b * BW, BW), BW)],
             field.at[b + 1, rows + 1, pl.ds(0, slices)],
-            halo_send.at[0, b],
+            halo_send.at[0],
             halo_recv.at[0, b],
             device_id=(above, place),
             device_id_type=MESH,
@@ -108,14 +112,14 @@
         return pltpu.make_async_remote_copy(
             density.at[rows - 1, :, pl.ds(pl.multiple_of(b * BW, BW), BW)],
             field.at[b + 1, 0, pl.ds(0, slices)],
-            halo_send.at[1, b],
+            halo_send.at[1],
             halo_recv.at[1, b],
             device_id=(below, place),
             device_id_type=MESH,
         )
 
     def start_halo(i, _):
-        b = turn(i)
+        b = block(i)
 
         @pl.when(has_above)
         def _():
@@ -127,13 +131,14 @@
 
         return 0
 
-    pl.semaphore_wait(barrier, nx * (2 * reach + 1) + jnp.where(jnp.logical_and(has_above, has_below), 1, 0))
-    for dz in (-reach, reach):
-        pl.semaphore_signal(near_sem, inc=1, device_id=at(x, along(dz)), device_id_type=MESH)
+    pl.semaphore_wait(barrier, nx * (2 * REACH + 1) + jnp.where(jnp.logical_and(has_above, has_below), 1, 0))
     lax.fori_loop(0, blocks, start_halo, 0)
-    pl.semaphore_wait(near_sem, 2)
-    for dz in (-NEAR, NEAR):
-        pl.semaphore_signal(far_sem, inc=1, device_id=at(x, along(dz)), device_id_type=MESH)
+    rounds = [REACH * 2**i for i in range((nz // 2 // REACH).bit_length() - 1)]
+    for i, far in enumerate(rounds):
+        if i:
+            pl.semaphore_wait(heard.at[i - 1], 2)
+        for dz in (-far, far):
+            pl.semaphore_signal(heard.at[i], inc=1, device_id=at(x, along(dz)), device_id_type=MESH)
 
     def end_load(b, _):
         load(b).wait()
@@ -178,14 +183,7 @@
         done = lax.fori_loop(0, slices, step, ((zero, one, zero),) * bricks, unroll=slices)
         return [(color, trans) for _, trans, color in done]
 
-    def r_copy(q, b):
-        return pltpu.make_async_remote_copy(
-            states.at[b, q], parts.at[place], r_send.at[b, q], r_recv, device_id=at(q, b), device_id_type=MESH
-        )
-
-    def one_block(i, _):
-        b = turn(i)
-
+    def marched(b):
         @pl.when(has_below)
         def _():
             halo_up(b).wait_recv()
@@ -194,26 +192,54 @@
         def _():
             halo_down(b).wait_recv()
 
-        for h, (color, trans) in enumerate(march(b)):
-            states[b, 2 * h] = jnp.where(upper, color, pltpu.roll(trans, HALF, 0))
-            states[b, 2 * h + 1] = jnp.where(upper, pltpu.roll(color, HALF, 0), trans)
-        return b
-
-    def sent_block(i, _):
-        b = one_block(i, 0)
-        for q in range(nx):
-            r_copy(q, b).start()
-        return 0
-
-    lax.fori_loop(0, 2 * NEAR, sent_block, 0)
-    pl.semaphore_wait(far_sem, 2)
-    lax.fori_loop(2 * NEAR, blocks - 1, sent_block, 0)
-    one_block(blocks - 1, 0)
-    for j in range(1, nx):
-        r_copy(lax.rem(x + j, nx), z).start()
-    parts[place] = states[z, x]
-
-    others = pl.ds(0, nx * nz - 1)
+        return march(b)
+
+    def s_copy(g):
+        return pltpu.make_async_remote_copy(
+            swap_out.at[g], swap_in.at[g], s_send, s_recv.at[g], device_id=at(x, partner), device_id_type=MESH
+        )
+
+    def for_partner(i, _):
+        g = turn(i)
+        for h, (color, trans) in enumerate(marched(2 * g + 1 - member)):
+            swap_out[g, 2 * h] = color
+            swap_out[g, 2 * h + 1] = trans
+        s_copy(g).start()
+        return 0
+
+    def r_copy(q, g):
+        return pltpu.make_async_remote_copy(
+            states.at[g, q], parts.at[x * groups + group], r_send, r_recv,
+            device_id=at(q, 2 * g + member), device_id_type=MESH,
+        )
+
+    in_front = member == 0
+
+    def for_owners(i, _):
+        g = turn(i)
+        mine = marched(2 * g + member)
+        s_copy(g).wait_recv()
+        for h, (color, trans) in enumerate(mine):
+            its_color, its_trans = swap_in[g, 2 * h], swap_in[g, 2 * h + 1]
+            color = jnp.where(in_front, color + trans * its_color, its_color + its_trans * color)
+            trans = trans * its_trans
+            states[g, 2 * h] = jnp.where(upper, color, pltpu.roll(trans, HALF, 0))
+            states[g, 2 * h + 1] = jnp.where(upper, pltpu.roll(color, HALF, 0), trans)
+        for j in range(1, nx):
+            r_copy(lax.rem(x + j, nx), g).start()
+
+        @pl.when(g != group)
+        def _():
+            r_copy(x, g).start()
+
+        return 0
+
+    lax.fori_loop(0, groups, for_partner, 0)
+    pl.semaphore_wait(heard.at[len(rounds) - 1], 2)
+    lax.fori_loop(0, groups, for_owners, 0)
+    parts[x * groups + group] = states[group, x]
+
+    others = pl.ds(0, nx * groups - 1)
     pltpu.make_async_remote_copy(
         parts.at[others], parts.at[others], o_sem, r_recv, device_id=at(lax.rem(x + 1, nx), z), device_id_type=MESH
     ).wait_recv()
@@ -224,7 +250,7 @@
         both = jnp.where(upper, pltpu.roll(part, HALF, 0), part)
         return color + trans * part, trans * both
 
-    color, trans = lax.fori_loop(0, nx * nz, over, (zero, one), unroll=nz)
+    color, trans = lax.fori_loop(0, nx * groups, over, (zero, one), unroll=nx * groups)
     pieces[x, z] = jnp.where(upper, color, trans)
 
     def g_copy(j):
@@ -249,6 +275,24 @@
     lax.fori_loop(0, nz - 1, start_g, 0)
     for j in range(1, nx):
         f_copy(j, z).start()
+
+    def sent(source, done):
+        pltpu.make_async_remote_copy(
+            source, source, done, done, device_id=(tile, place), device_id_type=MESH
+        ).wait_send()
+
+    every = field.at[pl.ds(0, blocks), 0, pl.ds(0, slices)]
+
+    @pl.when(has_above)
+    def _():
+        sent(every, halo_send.at[0])
+
+    @pl.when(has_below)
+    def _():
+        sent(every, halo_send.at[1])
+
+    sent(swap_out, s_send)
+    sent(parts.at[others], r_send)
 
     def pass_on(i, _):
         other = lax.rem(z + arrive(i), nz)
@@ -282,26 +326,10 @@
                 image[(c,) + spot] = emission[c] * color
             image[(3,) + spot] = 1.0 - trans
 
-    def end_halo(b, _):
-        @pl.when(has_above)
-        def _():
-            halo_up(b).wait_send()
-
-        @pl.when(has_below)
-        def _():
-            halo_down(b).wait_send()
-
-        for q in range(nx):
-            @pl.when(jnp.logical_or(q != x, b != z))
-            def _():
-                r_copy(q, b).wait_send()
-        return 0
-
     def end_g(j, _):
         g_copy(j).wait_send()
         return 0
 
-    lax.fori_loop(0, blocks, end_halo, 0)
     lax.fori_loop(1, nz, end_g, 0)
     for j in range(1, nx):
         whole(j).wait_send()
@@ -324,16 +352,19 @@
             pltpu.SMEM(extinction.shape, jnp.float32),
             pltpu.SMEM(edge_gain.shape, jnp.float32),
             pltpu.VMEM((blocks + 2, rows + 2, slices + PAD, BW), jnp.float32),
-            pltpu.VMEM((blocks, nx, BR, BW), jnp.float32),
-            pltpu.VMEM((nx * nz, BR, BW), jnp.float32),
+            pltpu.VMEM((nz // 2, 2 * rows // BR, BR, BW), jnp.float32),
+            pltpu.VMEM((nz // 2, 2 * rows // BR, BR, BW), jnp.float32),
+            pltpu.VMEM((nz // 2, nx, BR, BW), jnp.float32),
+            pltpu.VMEM((nx * nz // 2, BR, BW), jnp.float32),
             pltpu.VMEM((nx, nz, BR, BW), jnp.float32),
             dma((5,)),
             dma((blocks,)),
+            dma((2,)),
             dma((2, blocks)),
-            dma((2, blocks)),
-            plain,
-            plain,
-            dma((blocks, nx)),
+            plain(((nz // 2 // REACH).bit_length() - 1,)),
+            dma,
+            dma((nz // 2,)),
+            dma,
             dma,
             dma((nz,)),
             dma((nz,)),

time: 48.4 us -> 43.9 us (0.907)
  the two profiles are of different devices: /device:TPU:1 before, /device:TPU:8 now
where the time goes in v3:
time: 43.9 us; the launch traced here: 43.8 us
  Pallas kernels  41.7 us (95%)
  between operations  1.3 us (3%)
  local copies, waits for them, and re-layouts  0.8 us (2%)
    pallas_call x1, Pallas kernels, shards(): pl.pallas_call(functools.partial(render, nt, nx, nz), out_shape=pltpu.VME...  41.7 us

profile of v3, /device:TPU:8, one launch (start us, length us, event | category | flops | bytes accessed | tf_op | source)
XLA Modules:
  0.0 43.8 jit_solution(16016916108011478)
XLA Ops:
  1.3 41.7 %render.1 = f32[4,16,2048]{2,1,0:T(8,128)S(1)} custom-call(f32[16,32,2048]{2,1,0:T(8,128)} %density.1, s32[2,1,16]{2,1,0:T(1,128)} %start_in.1, s32[2,1,16]{2,1,0:T(1,128)} %count_in.1, f32[3]{0:T(128)} %emission_in.1, f32[1]{0:T(128)S(6)} %copy.9.extinction_in, f32[1]{0:T(128)S(6)} %copy.10.edge_gain_in), custom_call_target="tpu_custom_call" | custom-call | tf_op jit(solution)/shard_map/render/pallas_call | solution.py:343
  43.0 0.8 %copy.8 = f32[4,16,2048]{2,1,0:T(8,128)} copy(f32[4,16,2048]{2,1,0:T(8,128)S(1)} %render.1) | data formatting | bytes 1048576

commit v4 on v3

--- a/solution.py
+++ b/solution.py
@@ -14,6 +14,7 @@
 PAD = 8
 REACH = 2
 
+AHEAD = 2
 
 def render(
     nt, nx, nz, density, start_in, count_in, emission_in, extinction_in, edge_gain_in, image,
@@ -214,8 +215,9 @@
         )
 
     in_front = member == 0
-
-    def for_owners(i, _):
+    order = sorted(range(1, nx), key=lambda j: -min(j, nx - j))
+
+    def prepare(i, _):
         g = turn(i)
         mine = marched(2 * g + member)
         s_copy(g).wait_recv()
@@ -225,7 +227,11 @@
             trans = trans * its_trans
             states[g, 2 * h] = jnp.where(upper, color, pltpu.roll(trans, HALF, 0))
             states[g, 2 * h + 1] = jnp.where(upper, pltpu.roll(color, HALF, 0), trans)
-        for j in range(1, nx):
+        return 0
+
+    def hand_out(i, _):
+        g = turn(i)
+        for j in order:
             r_copy(lax.rem(x + j, nx), g).start()
 
         @pl.when(g != group)
@@ -234,9 +240,15 @@
 
         return 0
 
+    def for_owners(i, _):
+        prepare(i, 0)
+        return hand_out(i, 0)
+
     lax.fori_loop(0, groups, for_partner, 0)
+    lax.fori_loop(0, AHEAD, prepare, 0)
     pl.semaphore_wait(heard.at[len(rounds) - 1], 2)
-    lax.fori_loop(0, groups, for_owners, 0)
+    lax.fori_loop(0, AHEAD, hand_out, 0)
+    lax.fori_loop(AHEAD, groups, for_owners, 0)
     parts[x * groups + group] = states[group, x]
 
     others = pl.ds(0, nx * groups - 1)
@@ -255,7 +267,7 @@
 
     def g_copy(j):
         return pltpu.make_async_remote_copy(
-            pieces.at[x, z], pieces.at[x, z], g_send.at[j], g_recv.at[z], device_id=at(x, lax.rem(z + j, nz)), device_id_type=MESH
+            pieces.at[x, z], pieces.at[x, z], g_send, g_recv.at[z], device_id=at(x, lax.rem(z + j, nz)), device_id_type=MESH
         )
 
     def f_copy(j, other):
@@ -273,7 +285,7 @@
         return 0
 
     lax.fori_loop(0, nz - 1, start_g, 0)
-    for j in range(1, nx):
+    for j in order:
         f_copy(j, z).start()
 
     def sent(source, done):
@@ -297,14 +309,15 @@
     def pass_on(i, _):
         other = lax.rem(z + arrive(i), nz)
         pltpu.make_async_remote_copy(
-            pieces.at[x, other], pieces.at[x, other], g_send.at[other], g_recv.at[other],
+            pieces.at[x, other], pieces.at[x, other], g_send, g_recv.at[other],
             device_id=at(x, other), device_id_type=MESH,
         ).wait_recv()
-        for j in range(1, nx):
+        for j in order:
             f_copy(j, other).start()
         return 0
 
     lax.fori_loop(0, nz - 1, pass_on, 0)
+    sent(pieces.at[0, pl.ds(0, nz - 1)], g_send)
 
     def whole(j):
         other = lax.rem(x + j, nx)
@@ -326,11 +339,6 @@
                 image[(c,) + spot] = emission[c] * color
             image[(3,) + spot] = 1.0 - trans
 
-    def end_g(j, _):
-        g_copy(j).wait_send()
-        return 0
-
-    lax.fori_loop(1, nz, end_g, 0)
     for j in range(1, nx):
         whole(j).wait_send()
 
@@ -366,7 +374,7 @@
             dma((nz // 2,)),
             dma,
             dma,
-            dma((nz,)),
+            dma,
             dma((nz,)),
             dma((nx,)),
             dma((nx,)),

time: 43.9 us -> 43.6 us (level)
  the two profiles are of different devices: /device:TPU:8 before, /device:TPU:1 now
where the time goes in v4:
time: 43.6 us; the launch traced here: 43.4 us
  Pallas kernels  41.3 us (95%)
  between operations  1.3 us (3%)
  local copies, waits for them, and re-layouts  0.8 us (2%)
    pallas_call x1, Pallas kernels, shards(): pl.pallas_call(functools.partial(render, nt, nx, nz), out_shape=pltpu.VME...  41.3 us

profile of v4, /device:TPU:1, one launch (start us, length us, event | category | flops | bytes accessed | tf_op | source)
XLA Modules:
  0.0 43.4 jit_solution(7639496834508642142)
XLA Ops:
  1.3 41.3 %render.1 = f32[4,16,2048]{2,1,0:T(8,128)S(1)} custom-call(f32[16,32,2048]{2,1,0:T(8,128)} %density.1, s32[2,1,16]{2,1,0:T(1,128)} %start_in.1, s32[2,1,16]{2,1,0:T(1,128)} %count_in.1, f32[3]{0:T(128)} %emission_in.1, f32[1]{0:T(128)S(6)} %copy.9.extinction_in, f32[1]{0:T(128)S(6)} %copy.10.edge_gain_in), custom_call_target="tpu_custom_call" | custom-call | tf_op jit(solution)/shard_map/render/pallas_call | solution.py:351
  42.6 0.8 %copy.8 = f32[4,16,2048]{2,1,0:T(8,128)} copy(f32[4,16,2048]{2,1,0:T(8,128)S(1)} %render.1) | data formatting | bytes 1048576

commit v5 on v4

--- a/solution.py
+++ b/solution.py
@@ -12,13 +12,13 @@
 BR, BW = 8, 128
 HALF = BR // 2
 PAD = 8
-REACH = 2
-
-AHEAD = 2
+REACH = 4
+
+AHEAD = 7
 
 def render(
     nt, nx, nz, density, start_in, count_in, emission_in, extinction_in, edge_gain_in, image,
-    start, count, emission, extinction, edge_gain, field, swap_out, swap_in, states, parts, pieces,
+    start, count, emission, extinction, edge_gain, field, swap_out, swap_in, mine, states, parts, pieces,
     small_sem, load_sem, halo_send, halo_recv, heard, s_send, s_recv, r_send, r_recv, g_send, g_recv, f_send, f_recv, o_sem,
 ):
     rows, slices, width = density.shape
@@ -49,12 +49,11 @@
     def _():
         pl.semaphore_signal(barrier, inc=1, device_id=(below, place), device_id_type=MESH)
 
-    for dz in range(-REACH, REACH + 1):
-        for dx in range(nx):
-            if dx or dz:
-                pl.semaphore_signal(
-                    barrier, inc=1, device_id=at(lax.rem(x + dx, nx), along(dz)), device_id_type=MESH
-                )
+    near = [(dx, dz) for dx in range(nx) for dz in range(-REACH, REACH + 1) if dx or dz]
+    for dx, dz in sorted(near, key=lambda way: -min(way[0], nx - way[0]) - abs(way[1])):
+        pl.semaphore_signal(
+            barrier, inc=1, device_id=at(lax.rem(x + dx, nx), along(dz)), device_id_type=MESH
+        )
 
     small = [
         pltpu.make_async_copy(source, target, small_sem.at[i])
@@ -217,20 +216,23 @@
     in_front = member == 0
     order = sorted(range(1, nx), key=lambda j: -min(j, nx - j))
 
-    def prepare(i, _):
+    def for_self(i, _):
         g = turn(i)
-        mine = marched(2 * g + member)
+        for h, (color, trans) in enumerate(marched(2 * g + member)):
+            mine[g, 2 * h] = color
+            mine[g, 2 * h + 1] = trans
+        return 0
+
+    def hand_out(i, _):
+        g = turn(i)
         s_copy(g).wait_recv()
-        for h, (color, trans) in enumerate(mine):
+        for h in range(bricks):
+            color, trans = mine[g, 2 * h], mine[g, 2 * h + 1]
             its_color, its_trans = swap_in[g, 2 * h], swap_in[g, 2 * h + 1]
             color = jnp.where(in_front, color + trans * its_color, its_color + its_trans * color)
             trans = trans * its_trans
             states[g, 2 * h] = jnp.where(upper, color, pltpu.roll(trans, HALF, 0))
             states[g, 2 * h + 1] = jnp.where(upper, pltpu.roll(color, HALF, 0), trans)
-        return 0
-
-    def hand_out(i, _):
-        g = turn(i)
         for j in order:
             r_copy(lax.rem(x + j, nx), g).start()
 
@@ -241,11 +243,11 @@
         return 0
 
     def for_owners(i, _):
-        prepare(i, 0)
+        for_self(i, 0)
         return hand_out(i, 0)
 
     lax.fori_loop(0, groups, for_partner, 0)
-    lax.fori_loop(0, AHEAD, prepare, 0)
+    lax.fori_loop(0, AHEAD, for_self, 0)
     pl.semaphore_wait(heard.at[len(rounds) - 1], 2)
     lax.fori_loop(0, AHEAD, hand_out, 0)
     lax.fori_loop(AHEAD, groups, for_owners, 0)
@@ -360,6 +362,7 @@
             pltpu.SMEM(extinction.shape, jnp.float32),
             pltpu.SMEM(edge_gain.shape, jnp.float32),
             pltpu.VMEM((blocks + 2, rows + 2, slices + PAD, BW), jnp.float32),
+            pltpu.VMEM((nz // 2, 2 * rows // BR, BR, BW), jnp.float32),
             pltpu.VMEM((nz // 2, 2 * rows // BR, BR, BW), jnp.float32),
             pltpu.VMEM((nz // 2, 2 * rows // BR, BR, BW), jnp.float32),
             pltpu.VMEM((nz // 2, nx, BR, BW), jnp.float32),

time: 43.6 us -> 43.3 us (level)
  Pallas kernels: 41.3 us -> 40.8 us
    pallas_call x1, Pallas kernels: 41.3 us -> 40.8 us  [shards(): pl.pallas_call(functools.partial(render, nt, nx, nz), out_shape=pltpu.VME...]
where the time goes in v5:
time: 43.3 us; the launch traced here: 42.9 us
  Pallas kernels  40.8 us (94%)
  between operations  1.3 us (3%)
  local copies, waits for them, and re-layouts  0.8 us (2%)
    pallas_call x1, Pallas kernels, shards(): pl.pallas_call(functools.partial(render, nt, nx, nz), out_shape=pltpu.VME...  40.8 us

profile of v5, /device:TPU:1, one launch (start us, length us, event | category | flops | bytes accessed | tf_op | source)
XLA Modules:
  0.0 42.9 jit_solution(17607540725419949670)
XLA Ops:
  1.3 40.8 %render.1 = f32[4,16,2048]{2,1,0:T(8,128)S(1)} custom-call(f32[16,32,2048]{2,1,0:T(8,128)} %density.1, s32[2,1,16]{2,1,0:T(1,128)} %start_in.1, s32[2,1,16]{2,1,0:T(1,128)} %count_in.1, f32[3]{0:T(128)} %emission_in.1, f32[1]{0:T(128)S(6)} %copy.9.extinction_in, f32[1]{0:T(128)S(6)} %copy.10.edge_gain_in), custom_call_target="tpu_custom_call" | custom-call | tf_op jit(solution)/shard_map/render/pallas_call | solution.py:353
  42.1 0.8 %copy.8 = f32[4,16,2048]{2,1,0:T(8,128)} copy(f32[4,16,2048]{2,1,0:T(8,128)S(1)} %render.1) | data formatting | bytes 1048576

commit v6 on v5

--- a/solution.py
+++ b/solution.py
@@ -132,13 +132,14 @@
         return 0
 
     pl.semaphore_wait(barrier, nx * (2 * REACH + 1) + jnp.where(jnp.logical_and(has_above, has_below), 1, 0))
-    lax.fori_loop(0, blocks, start_halo, 0)
     rounds = [REACH * 2**i for i in range((nz // 2 // REACH).bit_length() - 1)]
     for i, far in enumerate(rounds):
         if i:
             pl.semaphore_wait(heard.at[i - 1], 2)
         for dz in (-far, far):
             pl.semaphore_signal(heard.at[i], inc=1, device_id=at(x, along(dz)), device_id_type=MESH)
+        if i == 0:
+            lax.fori_loop(0, blocks, start_halo, 0)
 
     def end_load(b, _):
         load(b).wait()

time: 43.3 us -> 43.3 us (level)
  no operation moved by 1% of the time
where the time goes in v6:
time: 43.3 us; the launch traced here: 42.9 us
  Pallas kernels  40.8 us (94%)
  between operations  1.3 us (3%)
  local copies, waits for them, and re-layouts  0.8 us (2%)
    pallas_call x1, Pallas kernels, shards(): pl.pallas_call(functools.partial(render, nt, nx, nz), out_shape=pltpu.VME...  40.8 us

profile of v6, /device:TPU:1, one launch (start us, length us, event | category | flops | bytes accessed | tf_op | source)
XLA Modules:
  0.0 42.9 jit_solution(2820431649682415344)
XLA Ops:
  1.3 40.8 %render.1 = f32[4,16,2048]{2,1,0:T(8,128)S(1)} custom-call(f32[16,32,2048]{2,1,0:T(8,128)} %density.1, s32[2,1,16]{2,1,0:T(1,128)} %start_in.1, s32[2,1,16]{2,1,0:T(1,128)} %count_in.1, f32[3]{0:T(128)} %emission_in.1, f32[1]{0:T(128)S(6)} %copy.9.extinction_in, f32[1]{0:T(128)S(6)} %copy.10.edge_gain_in), custom_call_target="tpu_custom_call" | custom-call | tf_op jit(solution)/shard_map/render/pallas_call | solution.py:354
  42.1 0.8 %copy.8 = f32[4,16,2048]{2,1,0:T(8,128)} copy(f32[4,16,2048]{2,1,0:T(8,128)S(1)} %render.1) | data formatting | bytes 1048576

commit v7 on v5

--- a/solution.py
+++ b/solution.py
@@ -15,6 +15,7 @@
 REACH = 4
 
 AHEAD = 7
+LATE = 4
 
 def render(
     nt, nx, nz, density, start_in, count_in, emission_in, extinction_in, edge_gain_in, image,
@@ -272,9 +273,9 @@
             pieces.at[x, z], pieces.at[x, z], g_send, g_recv.at[z], device_id=at(x, lax.rem(z + j, nz)), device_id_type=MESH
         )
 
-    def f_copy(j, other):
-        return pltpu.make_async_remote_copy(
-            pieces.at[x, other], pieces.at[x, other], f_send.at[j], f_recv.at[x],
+    def f_copy(j, other, wave):
+        return pltpu.make_async_remote_copy(
+            pieces.at[x, other], pieces.at[x, other], f_send.at[j], f_recv.at[wave, x],
             device_id=at(lax.rem(x + j, nx), z), device_id_type=MESH,
         )
 
@@ -288,7 +289,7 @@
 
     lax.fori_loop(0, nz - 1, start_g, 0)
     for j in order:
-        f_copy(j, z).start()
+        f_copy(j, z, 0).start()
 
     def sent(source, done):
         pltpu.make_async_remote_copy(
@@ -315,7 +316,7 @@
             device_id=at(x, other), device_id_type=MESH,
         ).wait_recv()
         for j in order:
-            f_copy(j, other).start()
+            f_copy(j, other, jnp.where(i < nz - 1 - LATE, 0, 1)).start()
         return 0
 
     lax.fori_loop(0, nz - 1, pass_on, 0)
@@ -324,22 +325,37 @@
     def whole(j):
         other = lax.rem(x + j, nx)
         return pltpu.make_async_remote_copy(
-            pieces.at[other], pieces.at[other], f_send.at[j], f_recv.at[other],
+            pieces.at[other], pieces.at[other], f_send.at[j], f_recv.at[0, other],
             device_id=at(other, z), device_id_type=MESH,
         )
 
-    for j in range(1, nx):
-        whole(j).wait_recv()
-
-    for b in range(blocks):
+    def landed(count, wave):
+        for j in range(1, nx):
+            some = pieces.at[0, pl.ds(0, count)]
+            pltpu.make_async_remote_copy(
+                some, some, f_send.at[j], f_recv.at[wave, lax.rem(x + j, nx)],
+                device_id=at(lax.rem(x + j, nx), z), device_id_type=MESH,
+            ).wait_recv()
+
+    def assemble(b):
         for h in range(bricks):
             first, second = pieces[2 * h, b], pieces[2 * h + 1, b]
             color = jnp.where(upper, first, pltpu.roll(second, HALF, 0))
             trans = jnp.where(upper, pltpu.roll(first, HALF, 0), second)
-            spot = (pl.ds(BR * h, BR), pl.ds(BW * b, BW))
+            spot = (pl.ds(BR * h, BR), pl.ds(pl.multiple_of(BW * b, BW), BW))
             for c in range(3):
                 image[(c,) + spot] = emission[c] * color
             image[(3,) + spot] = 1.0 - trans
+
+    def picture(i, _):
+        assemble(lax.rem(z + arrive(i), nz))
+        return 0
+
+    landed(nz - LATE, 0)
+    assemble(z)
+    lax.fori_loop(0, nz - 1 - LATE, picture, 0)
+    landed(LATE, 1)
+    lax.fori_loop(nz - 1 - LATE, nz - 1, picture, 0, unroll=LATE)
 
     for j in range(1, nx):
         whole(j).wait_send()
@@ -380,7 +396,7 @@
             dma,
             dma((nz,)),
             dma((nx,)),
-            dma((nx,)),
+            dma((2, nx)),
             dma,
         ],
         compiler_params=pltpu.CompilerParams(

time: 43.3 us -> 43.3 us (level)
  no operation moved by 1% of the time
where the time goes in v7:
time: 43.3 us; the launch traced here: 42.9 us
  Pallas kernels  40.8 us (94%)
  between operations  1.3 us (3%)
  local copies, waits for them, and re-layouts  0.8 us (2%)
    pallas_call x1, Pallas kernels, shards(): pl.pallas_call(functools.partial(render, nt, nx, nz), out_shape=pltpu.VME...  40.8 us

profile of v7, /device:TPU:1, one launch (start us, length us, event | category | flops | bytes accessed | tf_op | source)
XLA Modules:
  0.0 42.9 jit_solution(2996372057549291593)
XLA Ops:
  1.3 40.8 %render.1 = f32[4,16,2048]{2,1,0:T(8,128)S(1)} custom-call(f32[16,32,2048]{2,1,0:T(8,128)} %density.1, s32[2,1,16]{2,1,0:T(1,128)} %start_in.1, s32[2,1,16]{2,1,0:T(1,128)} %count_in.1, f32[3]{0:T(128)} %emission_in.1, f32[1]{0:T(128)S(6)} %copy.9.extinction_in, f32[1]{0:T(128)S(6)} %copy.10.edge_gain_in), custom_call_target="tpu_custom_call" | custom-call | tf_op jit(solution)/shard_map/render/pallas_call | solution.py:369
  42.1 0.8 %copy.8 = f32[4,16,2048]{2,1,0:T(8,128)} copy(f32[4,16,2048]{2,1,0:T(8,128)S(1)} %render.1) | data formatting | bytes 1048576
